TPU v7x, 32 devices: a whole 2x2x4 slice. The times are simulated.
32 devices in a mesh: dp: 8 (over z, x), fsdp: 4 (over y, core).
Axes of the slice: x: 2, y: 2, z: 4, core: 2. Of those that a mesh axis runs over, the one named last changes fastest.
Arguments:
- tokens: bfloat16 [640, 197, 384], P(('dp', 'fsdp')), may hold values from -6 to 6
- image_count: int32 [32], P(('dp', 'fsdp')), may hold values from 1 to 20, as said below
- w_qkv: bfloat16 [442368], P(('dp', 'fsdp')), may hold values from -0.3125 to 0.3125
- w_out: bfloat16 [147456], P(('dp', 'fsdp')), may hold values from -1.25 to 1.25
- w_fc1: bfloat16 [589824], P(('dp', 'fsdp')), may hold values from -0.3125 to 0.3125
- w_fc2: bfloat16 [589824], P(('dp', 'fsdp')), may hold values from -0.15625 to 0.15625
- norm_bias: bfloat16 [4608], P(('dp', 'fsdp')), may hold values from -1.5 to 1.5, as said below
- cotangent: bfloat16 [640, 197, 384], P(('dp', 'fsdp')), may hold values from -6 to 6
Outputs:
- output: bfloat16 [640, 197, 384], P(('dp', 'fsdp'))
- grad_tokens: bfloat16 [640, 197, 384], P(('dp', 'fsdp'))
- grad_qkv: float32 [442368], P(('dp', 'fsdp'))
- grad_out: float32 [147456], P(('dp', 'fsdp'))
- grad_fc1: float32 [589824], P(('dp', 'fsdp'))
- grad_fc2: float32 [589824], P(('dp', 'fsdp'))
- grad_norm_bias: float32 [4608], P(('dp', 'fsdp'))
Inputs may be any that keep to these rules, and one draw needn't show every extreme that they name: `image_count`: live images among a device's 20 slots, the first ones; some device holds 20. `norm_bias`: gains near one, biases and shifts of either sign.
All inputs are finite; a program needn't handle non-finite values.
Results may differ from a plain program's by a relative error of at most 0.011.
Values may be sent and summed in bfloat16 or wider, within the bound.
A program may use at most 256 MiB of HBM per device.

v0:
```python
import functools
import math

import jax
import jax.numpy as jnp
from jax import lax
from jax.experimental import pallas as pl
from jax.experimental.pallas import tpu as pltpu
from jax.sharding import PartitionSpec as P

HEADS = 6
HEAD_DIM = 64
EPS = 1e-06
F32 = jnp.float32
BF16 = jnp.bfloat16


def mm(a, b):
    return lax.dot_general(a, b, (((1,), (0,)), ((), ())), preferred_element_type=F32)


def mm_t(a, b):
    return lax.dot_general(a, b, (((1,), (1,)), ((), ())), preferred_element_type=F32)


def t_mm(a, b):
    return lax.dot_general(a, b, (((0,), (0,)), ((), ())), preferred_element_type=F32)


def norm_parts(values, width):
    mean = jnp.sum(values, axis=-1, keepdims=True) * (1.0 / width)
    center = values - mean
    var = jnp.sum(center * center, axis=-1, keepdims=True) * (1.0 / width)
    inverse = lax.rsqrt(var + EPS)
    return center * inverse, inverse


def norm_back(upstream, normed, inverse, gain, width):
    scaled = upstream * gain
    m1 = jnp.sum(scaled, axis=-1, keepdims=True) * (1.0 / width)
    m2 = jnp.sum(scaled * normed, axis=-1, keepdims=True) * (1.0 / width)
    return inverse * (scaled - m1 - normed * m2)


def gelu_both(z):
    ez = jnp.exp2(z * z * (-0.5 * 1.4426950408889634))
    d = 1.0 + (0.3275911 * 0.7071067811865476) * jnp.abs(z)
    t = pl.reciprocal(d, approx=True)
    t = t * (2.0 - d * t)
    poly = (((0.5307027145 * t - 0.7265760135) * t + 0.7107068705) * t - 0.142248368) * t + 0.127414796
    half = poly * t * ez
    cumul = jnp.where(z >= 0.0, 1.0 - half, half)
    return z * cumul, cumul + z * (ez * 0.3989422804014327)


def layer_kernel(
    count_ref, x_ref, ct_ref, wqkv_ref, wout_ref, wup_ref, wdown_ref, small_ref, bup_ref,
    out_ref, gx_ref, oqkv_ref, oout_ref, oup_ref, odown_ref, gsmall_ref, gbup_ref,
    gqkv_ref, gout_ref, gup_ref, gdown_ref,
    xs, cs, n1s, qs, ks, vs, pbs, os_, y1s, n2s, a1s, a2s, acts, dzs, dos, dqkvs,
):
    step = pl.program_id(0)
    seq, width = x_ref.shape[1], x_ref.shape[2]
    rows = xs.shape[0]
    hidden = wup_ref.shape[1]
    scale = 1.0 / math.sqrt(HEAD_DIM)

    @pl.when(step == 0)
    def _():
        xs[...] = jnp.zeros_like(xs)
        cs[...] = jnp.zeros_like(cs)
        for ref in (gqkv_ref, gout_ref, gup_ref, gdown_ref, gsmall_ref, gbup_ref):
            ref[...] = jnp.zeros_like(ref)

    live = step < count_ref[0]

    @pl.when(jnp.logical_not(live))
    def _():
        out_ref[...] = jnp.zeros_like(out_ref)
        gx_ref[...] = jnp.zeros_like(gx_ref)

    @pl.when(live)
    def _():
        xs[0:seq, :] = x_ref[0]
        cs[0:seq, :] = ct_ref[0]
        g1, c1 = small_ref[0:1, :], small_ref[1:2, :]
        bq, bv, bo = small_ref[2:3, :], small_ref[3:4, :], small_ref[4:5, :]
        g2, c2, b2 = small_ref[5:6, :], small_ref[6:7, :], small_ref[7:8, :]
        n1, inv1 = norm_parts(xs[...].astype(F32), width)
        n1s[...] = n1
        a1s[...] = (n1 * g1 + c1).astype(BF16)
        qs[...] = ((mm(a1s[...], wqkv_ref[:, :width]) + bq).astype(BF16).astype(F32) * scale).astype(BF16)
        ks[...] = mm(a1s[...], wqkv_ref[:, width : 2 * width]).astype(BF16)
        vs[...] = (mm(a1s[...], wqkv_ref[:, 2 * width :]) + bv).astype(BF16)
        lane = lax.broadcasted_iota(jnp.int32, (rows, 2 * HEAD_DIM), 1)
        halves = (lane < HEAD_DIM, lane >= HEAD_DIM)
        whole_rows = seq // 8 * 8
        keyrow = whole_rows + lax.broadcasted_iota(jnp.int32, (rows - whole_rows, rows), 0)
        zero = jnp.zeros((rows, 2 * HEAD_DIM), BF16)
        for pair in range(HEADS // 2):
            cols = slice(pair * 2 * HEAD_DIM, (pair + 1) * 2 * HEAD_DIM)
            qp, kp, vp = qs[:, cols], ks[:, cols], vs[:, cols]
            both = None
            for h in range(2):
                km = jnp.where(halves[h], kp, zero)
                vm = jnp.where(halves[h], vp, zero)
                scores = mm_t(km, qp)
                scores = jnp.concatenate(
                    [scores[:whole_rows], jnp.where(keyrow < seq, scores[whole_rows:], -1e30)], axis=0
                )
                top = jnp.max(scores, axis=0, keepdims=True)
                expo = jnp.exp(scores - top)
                total = jnp.sum(expo, axis=0, keepdims=True)
                prob = expo * (1.0 / total)
                pbs[pair * 2 + h] = prob.astype(BF16)
                part = t_mm(pbs[pair * 2 + h], vm)
                both = part if both is None else both + part
            os_[:, cols] = both.astype(BF16)
        y1 = xs[...].astype(F32) + (mm(os_[...], wout_ref[...]) + bo)
        y1s[...] = y1
        n2, inv2 = norm_parts(y1, width)
        n2s[...] = n2
        a2s[...] = (n2 * g2 + c2).astype(BF16)
        tile = 256
        for j in range(hidden // tile):
            cols = slice(j * tile, (j + 1) * tile)
            z = mm(a2s[...], wup_ref[:, cols]) + bup_ref[:, cols]
            act, slope = gelu_both(z)
            acts[:, cols] = act.astype(BF16)
            dz = (mm_t(cs[...], wdown_ref[cols, :]) * slope).astype(BF16)
            dzs[:, cols] = dz
            gbup_ref[:, cols] += jnp.sum(dz.astype(F32), axis=0, keepdims=True)
        y = y1s[...] + mm(acts[...], wdown_ref[...]) + b2
        out_ref[0] = y[:seq].astype(BF16)
        gdown_ref[...] += t_mm(cs[...], acts[...])
        gup_ref[...] += t_mm(a2s[...], dzs[...])
        da2 = mm_t(dzs[...], wup_ref[...])
        ct = cs[...].astype(F32)
        n2 = n2s[...]
        gsmall_ref[7:8, :] += jnp.sum(ct, axis=0, keepdims=True)
        gsmall_ref[5:6, :] += jnp.sum(da2 * n2, axis=0, keepdims=True)
        gsmall_ref[6:7, :] += jnp.sum(da2, axis=0, keepdims=True)
        dy1 = ct + norm_back(da2, n2, inv2, g2, width)
        y1s[...] = dy1
        da = dy1.astype(BF16)
        gsmall_ref[4:5, :] += jnp.sum(da.astype(F32), axis=0, keepdims=True)
        gout_ref[...] += t_mm(os_[...], da)
        dos[...] = mm_t(da, wout_ref[...]).astype(BF16)
        for pair in range(HEADS // 2):
            cols = slice(pair * 2 * HEAD_DIM, (pair + 1) * 2 * HEAD_DIM)
            qp, kp, vp, dop = qs[:, cols], ks[:, cols], vs[:, cols], dos[:, cols]
            dq = dk = dv = None
            for h in range(2):
                qm = jnp.where(halves[h], qp, zero)
                km = jnp.where(halves[h], kp, zero)
                vm = jnp.where(halves[h], vp, zero)
                dom = jnp.where(halves[h], dop, zero)
                pb = pbs[pair * 2 + h]
                prob = pb.astype(F32)
                dp = mm_t(vm, dop)
                inner = jnp.sum(prob * dp, axis=0, keepdims=True)
                ds = (prob * (dp - inner)).astype(BF16)
                dv_h = mm(pb, dom)
                dk_h = mm(ds, qm)
                dq_h = t_mm(ds, km)
                dq = dq_h if dq is None else dq + dq_h
                dk = dk_h if dk is None else dk + dk_h
                dv = dv_h if dv is None else dv + dv_h
            base = pair * 2 * HEAD_DIM
            dqkvs[:, base : base + 2 * HEAD_DIM] = (dq * scale).astype(BF16)
            dqkvs[:, width + base : width + base + 2 * HEAD_DIM] = dk.astype(BF16)
            dqkvs[:, 2 * width + base : 2 * width + base + 2 * HEAD_DIM] = dv.astype(BF16)
        gsmall_ref[2:3, :] += jnp.sum(dqkvs[:, :width].astype(F32), axis=0, keepdims=True)
        gsmall_ref[3:4, :] += jnp.sum(dqkvs[:, 2 * width :].astype(F32), axis=0, keepdims=True)
        gqkv_ref[...] += t_mm(a1s[...], dqkvs[...])
        da1 = mm_t(dqkvs[...], wqkv_ref[...])
        n1 = n1s[...]
        gsmall_ref[0:1, :] += jnp.sum(da1 * n1, axis=0, keepdims=True)
        gsmall_ref[1:2, :] += jnp.sum(da1, axis=0, keepdims=True)
        gx = y1s[...] + norm_back(da1, n1, inv1, g1, width)
        gx_ref[0] = gx[:seq].astype(BF16)

    @pl.when(step == pl.num_programs(0) - 1)
    def _():
        oqkv_ref[...] = gqkv_ref[...].astype(BF16)
        oout_ref[...] = gout_ref[...].astype(BF16)
        oup_ref[...] = gup_ref[...].astype(BF16)
        for j in range(hidden // width):
            block = slice(j * width, (j + 1) * width)
            odown_ref[block, :] = gdown_ref[:, block].T.astype(BF16)


def run_layer(count, tokens, cotangent, wqkv, wout, wup, wdown, small, bup):
    slots, seq, width = tokens.shape
    hidden = wup.shape[1]
    rows = (seq + 15) // 16 * 16

    def whole(shape):
        return pl.BlockSpec(shape, lambda i, c: (0,) * len(shape), pipeline_mode=pl.Buffered(1))

    def image():
        return pl.BlockSpec((1, seq, width), lambda i, c: (i, 0, 0))

    return pl.pallas_call(
        layer_kernel,
        grid_spec=pltpu.PrefetchScalarGridSpec(
            num_scalar_prefetch=1,
            grid=(slots,),
            in_specs=[
                image(), image(),
                whole((width, 3 * width)), whole((width, width)), whole((width, hidden)),
                whole((hidden, width)), whole((8, width)), whole((1, hidden)),
            ],
            out_specs=[
                image(), image(),
                whole((width, 3 * width)), whole((width, width)), whole((width, hidden)),
                whole((hidden, width)), whole((8, width)), whole((1, hidden)),
            ],
            scratch_shapes=[
                pltpu.VMEM((width, 3 * width), F32),
                pltpu.VMEM((width, width), F32),
                pltpu.VMEM((width, hidden), F32),
                pltpu.VMEM((width, hidden), F32),
                pltpu.VMEM((rows, width), BF16),
                pltpu.VMEM((rows, width), BF16),
                pltpu.VMEM((rows, width), F32),
                pltpu.VMEM((rows, width), BF16),
                pltpu.VMEM((rows, width), BF16),
                pltpu.VMEM((rows, width), BF16),
                pltpu.VMEM((HEADS, rows, rows), BF16),
                pltpu.VMEM((rows, width), BF16),
                pltpu.VMEM((rows, width), F32),
                pltpu.VMEM((rows, width), F32),
                pltpu.VMEM((rows, width), BF16),
                pltpu.VMEM((rows, width), BF16),
                pltpu.VMEM((rows, hidden), BF16),
                pltpu.VMEM((rows, hidden), BF16),
                pltpu.VMEM((rows, width), BF16),
                pltpu.VMEM((rows, 3 * width), BF16),
            ],
        ),
        out_shape=[
            jax.ShapeDtypeStruct(tokens.shape, BF16),
            jax.ShapeDtypeStruct(tokens.shape, BF16),
            jax.ShapeDtypeStruct((width, 3 * width), BF16),
            jax.ShapeDtypeStruct((width, width), BF16),
            jax.ShapeDtypeStruct((width, hidden), BF16),
            jax.ShapeDtypeStruct((hidden, width), BF16),
            jax.ShapeDtypeStruct((8, width), F32),
            jax.ShapeDtypeStruct((1, hidden), F32),
        ],
        compiler_params=pltpu.CompilerParams(
            dimension_semantics=("arbitrary",), vmem_limit_bytes=48 * 1024 * 1024
        ),
    )(count, tokens, cotangent, wqkv, wout, wup, wdown, small, bup)


MESH = pl.DeviceIdType.MESH
CORES = 2
LANES = 128


def greet(n_dp, n_y, dp, y, core):
    barrier = pltpu.get_barrier_semaphore()
    pl.semaphore_signal(
        barrier, inc=1, device_id=(dp, y * CORES + 1 - core), device_id_type=MESH
    )
    for k in range(1, n_y):
        other = lax.rem(y + k, n_y)
        pl.semaphore_signal(barrier, inc=1, device_id=(dp, other * CORES + core), device_id_type=MESH)
    for k in range(1, n_dp):
        other = lax.rem(dp + k, n_dp)
        pl.semaphore_signal(barrier, inc=1, device_id=(other, y * CORES + core), device_id_type=MESH)
    pl.semaphore_wait(barrier, n_dp + n_y - 1)


def gather_kernel(n_dp, n_y, count, *refs):
    parts, (o_ref, x_ref, own_sem, dp_send, y_send, core_send, recv_sem) = refs[:count], refs[count:]
    fill(x_ref, parts)
    dp = lax.axis_index("dp")
    place = lax.axis_index("fsdp")
    y, core = place // CORES, lax.rem(place, CORES)
    n_f = n_y * CORES
    greet(n_dp, n_y, dp, y, core)
    me = dp * n_f + place
    sent = []

    def send(src, slot, sem, device):
        copy = pltpu.make_async_remote_copy(
            src_ref=src, dst_ref=o_ref.at[slot], send_sem=sem, recv_sem=recv_sem.at[slot],
            device_id=device, device_id_type=MESH,
        )
        copy.start()
        sent.append(copy)

    def arrived(slot):
        pltpu.make_async_remote_copy(
            src_ref=x_ref, dst_ref=o_ref.at[slot], send_sem=own_sem, recv_sem=recv_sem.at[slot],
            device_id=(dp, y * CORES + 1 - core), device_id_type=MESH,
        ).wait_recv()

    own = pltpu.make_async_copy(x_ref, o_ref.at[me], own_sem)
    own.start()
    for k in range(1, n_dp):
        send(x_ref, me, dp_send.at[k], (lax.rem(dp + k, n_dp), place))
    for j in range(n_dp):
        slot = lax.rem(dp + n_dp - j, n_dp) * n_f + place
        if j:
            arrived(slot)
        src = o_ref.at[slot] if j else x_ref
        for k in range(1, n_y):
            send(src, slot, y_send.at[j, k], (dp, lax.rem(y + k, n_y) * CORES + core))
        send(src, slot, core_send.at[j, 0], (dp, y * CORES + 1 - core))
    for j in range(n_dp):
        for k in range(1, n_y):
            slot = lax.rem(dp + n_dp - j, n_dp) * n_f + lax.rem(y + n_y - k, n_y) * CORES + core
            arrived(slot)
            send(o_ref.at[slot], slot, core_send.at[j, k], (dp, y * CORES + 1 - core))
    for j in range(n_dp):
        for k in range(n_y):
            slot = lax.rem(dp + n_dp - j, n_dp) * n_f + lax.rem(y + n_y - k, n_y) * CORES + 1 - core
            arrived(slot)
    own.wait()
    for copy in sent:
        copy.wait_send()


def fill(block, parts):
    at = 0
    for part in parts:
        block[at : at + part.shape[0], :] = part[...]
        at += tall(part.shape[0])


def gather_all(parts, n_dp, n_f):
    n_y = n_f // CORES
    height = sum(tall(p.shape[0]) for p in parts)
    block = (height, LANES)
    return pl.pallas_call(
        lambda *refs: gather_kernel(n_dp, n_y, len(parts), *refs),
        out_shape=jax.ShapeDtypeStruct((n_dp * n_f, *block), BF16),
        in_specs=[pl.BlockSpec(memory_space=pltpu.VMEM)] * len(parts),
        out_specs=pl.BlockSpec(memory_space=pl.ANY),
        scratch_shapes=[
            pltpu.VMEM(block, BF16),
            pltpu.SemaphoreType.DMA,
            pltpu.SemaphoreType.DMA((n_dp,)),
            pltpu.SemaphoreType.DMA((n_dp, n_y)),
            pltpu.SemaphoreType.DMA((n_dp, n_y)),
            pltpu.SemaphoreType.DMA((n_dp * n_f,)),
        ],
        compiler_params=pltpu.CompilerParams(collective_id=0, has_side_effects=True),
    )(*parts)


def scatter_kernel(n_dp, n_y, count, *refs):
    parts, outs = refs[:count], refs[count : 2 * count]
    g_ref, o_ref, r1, a1, r2, a2, r3, s1, s2, s3, q1, q2, q3 = refs[2 * count :]

    def fill_slot(slot, carry):
        at = 0
        for part in parts:
            g_ref[slot, at : at + part.shape[1], :] = part[slot]
            at += tall(part.shape[1])
        return carry

    lax.fori_loop(0, n_dp * n_y * CORES, fill_slot, 0)
    dp = lax.axis_index("dp")
    place = lax.axis_index("fsdp")
    y, core = place // CORES, lax.rem(place, CORES)
    n_f = n_y * CORES
    greet(n_dp, n_y, dp, y, core)
    sibling = (dp, y * CORES + 1 - core)
    sent = []

    def send(src, dst, ssem, rsem, device):
        copy = pltpu.make_async_remote_copy(
            src_ref=src, dst_ref=dst, send_sem=ssem, recv_sem=rsem,
            device_id=device, device_id_type=MESH,
        )
        copy.start()
        sent.append(copy)

    def arrived(dst, rsem):
        pltpu.make_async_remote_copy(
            src_ref=dst, dst_ref=dst, send_sem=s1.at[0, 0], recv_sem=rsem,
            device_id=sibling, device_id_type=MESH,
        ).wait_recv()

    order = list(range(1, n_dp)) + [0]
    hops = list(range(1, n_y)) + [0]

    def target(j):
        return lax.rem(dp + j, n_dp)

    def column(k):
        return lax.rem(y + k, n_y)

    for k in hops:
        for j in order:
            slot = target(j) * n_f + column(k) * CORES + 1 - core
            send(g_ref.at[slot], r1.at[j, k], s1.at[j, k], q1.at[j, k], sibling)
    for k in hops[:-1]:
        for j in order:
            arrived(r1.at[j, k], q1.at[j, k])
            slot = target(j) * n_f + column(k) * CORES + core
            a1[j, k - 1] = (g_ref[slot].astype(F32) + r1[j, k].astype(F32)).astype(BF16)
            send(a1.at[j, k - 1], r2.at[j, k - 1], s2.at[j, k - 1], q2.at[j, k - 1],
                 (dp, column(k) * CORES + core))
    for j in order:
        arrived(r1.at[j, 0], q1.at[j, 0])
        slot = target(j) * n_f + place
        total = g_ref[slot].astype(F32) + r1[j, 0].astype(F32)
        for k in hops[:-1]:
            arrived(r2.at[j, k - 1], q2.at[j, k - 1])
            total = total + r2[j, k - 1].astype(F32)
        if j:
            a2[j - 1] = total.astype(BF16)
            send(a2.at[j - 1], r3.at[j - 1], s3.at[j - 1], q3.at[j - 1], (target(j), place))
        else:
            o_ref[...] = total
    for j in order[:-1]:
        arrived(r3.at[j - 1], q3.at[j - 1])
        o_ref[...] += r3[j - 1].astype(F32)
    at = 0
    for out in outs:
        out[...] = o_ref[at : at + out.shape[0], :]
        at += tall(out.shape[0])
    for copy in sent:
        copy.wait_send()


def scatter_sum(terms, n_dp, n_f):
    n_y = n_f // CORES
    block = (sum(tall(t.shape[1]) for t in terms), LANES)
    far = max(n_y - 1, 1)
    dma = pltpu.SemaphoreType.DMA
    return pl.pallas_call(
        lambda *refs: scatter_kernel(n_dp, n_y, len(terms), *refs),
        out_shape=[jax.ShapeDtypeStruct(t.shape[1:], F32) for t in terms],
        in_specs=[pl.BlockSpec(memory_space=pltpu.VMEM)] * len(terms),
        out_specs=[pl.BlockSpec(memory_space=pltpu.VMEM)] * len(terms),
        scratch_shapes=[
            pltpu.VMEM((n_dp * n_f, *block), BF16),
            pltpu.VMEM(block, F32),
            pltpu.VMEM((n_dp, n_y, *block), BF16),
            pltpu.VMEM((n_dp, far, *block), BF16),
            pltpu.VMEM((n_dp, far, *block), BF16),
            pltpu.VMEM((n_dp - 1, *block), BF16),
            pltpu.VMEM((n_dp - 1, *block), BF16),
            dma((n_dp, n_y)), dma((n_dp, far)), dma((n_dp - 1,)),
            dma((n_dp, n_y)), dma((n_dp, far)), dma((n_dp - 1,)),
        ],
        compiler_params=pltpu.CompilerParams(
            collective_id=1, has_side_effects=True, vmem_limit_bytes=40 * 1024 * 1024
        ),
    )(*terms)


def lanes_of(size):
    return (size + LANES - 1) // LANES


def to_rows(values, count):
    flat = values.reshape(count, -1)
    size = flat.shape[1]
    if size % LANES:
        flat = jnp.pad(flat, ((0, 0), (0, lanes_of(size) * LANES - size)))
    else:
        flat = values
    return flat.reshape(count, lanes_of(size), LANES)


def tall(height):
    return (height + 15) // 16 * 16


def unpack(rows, sizes):
    outs, at = [], 0
    for size in sizes:
        height = lanes_of(size)
        piece = rows[:, at : at + height]
        if size % LANES:
            piece = piece.reshape(rows.shape[0], height * LANES)[:, :size]
        outs.append(piece)
        at += tall(height)
    return outs


def body(n_dp, n_f, tokens, image_count, w_qkv, w_out, w_fc1, w_fc2, norm_bias, cotangent):
    slots, seq, width = tokens.shape
    shards = (w_qkv, w_out, w_fc1, w_fc2, norm_bias)
    sizes = [s.shape[0] for s in shards]
    devices = n_dp * n_f
    gathered = gather_all([to_rows(p, 1)[0] for p in shards], n_dp, n_f)
    parts = unpack(gathered, sizes)
    hidden = sizes[2] * devices // width
    wqkv = parts[0].reshape(width, 3 * width)
    wout = parts[1].reshape(width, width)
    wup = parts[2].reshape(width, hidden)
    wdown = parts[3].reshape(hidden, width)
    vec = parts[4].astype(F32).reshape(-1)
    small = jnp.concatenate([vec[: 7 * width], vec[7 * width + hidden :]]).reshape(8, width)
    bup = vec[7 * width : 7 * width + hidden].reshape(1, hidden)
    output, grad_tokens, gqkv, gout, gup, gdown, gsmall, gbup = run_layer(
        image_count, tokens, cotangent, wqkv, wout, wup, wdown, small, bup
    )
    flat = gsmall.reshape(-1)
    gvec = jnp.concatenate([flat[: 7 * width], gbup.reshape(-1), flat[7 * width :]]).astype(BF16)
    terms = [to_rows(g, devices) for g in (gqkv, gout, gup, gdown, gvec)]
    summed = scatter_sum(terms, n_dp, n_f)
    grads = [g.reshape(-1)[:size] for g, size in zip(summed, sizes)]
    return (output, grad_tokens, *grads)


def solution(mesh):
    both = P(("dp", "fsdp"))
    images = P(("dp", "fsdp"), None, None)
    sizes = (mesh.shape["dp"], mesh.shape["fsdp"])
    return jax.shard_map(
        functools.partial(body, *sizes),
        mesh=mesh,
        in_specs=(images, both, both, both, both, both, both, images),
        out_specs=(images, images, both, both, both, both, both),
        check_vma=False,
    )
```

profile of v0, /device:TPU:11, one launch (start us, length us, event | category | flops | bytes accessed | tf_op | source)
XLA Modules:
  0.0 244.6 jit_solution(8981361658035438917)
XLA Ops:
  1.3 0.7 reshape.86
  1.9 0.5 pad_reduce_fusion
  2.5 35.0 %shard_map.135 = bf16[32,464,128]{2,1,0:T(8,128)(2,1)} custom-call(bf16[108,128]{1,0:T(8,128)(2,1)} %bitcast.26, bf16[36,128]{1,0:T(8,128)(2,1)} %bitcast.27, bf16[144,128]{1,0:T(8,128)(2,1)} %bitcast.23, bf16[144,128]{1,0:T(8,128)(2,1)} %bitcast.24, bf16[2,128]{1,0:T(2,128)(2,1)} %bitcast.28), custom_call_target="tpu_custom_call" | custom-call | tf_op jit(solution)/shard_map/pallas_call | solution.py:339
  37.5 0.9 slice.48
  38.4 0.1 reshape.108
  38.5 0.6 reshape.95.bup_ref
  39.1 1.0 slice.45
  40.1 0.2 reshape.88.wout_ref
  40.3 0.0 slice-start
  40.3 2.9 %fusion = (bf16[32,144,128]{2,1,0:T(8,128)(2,1)S(1)}, bf16[32,144,128]{2,1,0:T(8,128)(2,1)}) fusion(bf16[32,464,128]{2,1,0:T(8,128)(2,1)} %shard_map.135), kind=kLoop, calls=%fused_computation.7 | loop fusion | bytes 4718592 | tf_op jit(solution)/shard_map/slice | solution.py:482
  43.2 1.0 reshape.87.wqkv_ref
  44.2 0.0 copy-start.5
  44.2 1.6 reshape.90.wdown_ref
  45.8 1.4 reshape.89.wup_ref
  47.2 0.0 copy-start.4
  47.2 0.7 copy-done.4
  47.9 96.3 %shard_map.136 = (bf16[20,197,384]{2,1,0:T(8,128)(2,1)}, bf16[20,197,384]{2,1,0:T(8,128)(2,1)}, bf16[384,1152]{1,0:T(8,128)(2,1)S(1)}, bf16[384,384]{1,0:T(8,128...) custom-call(s32[1]{0:T(128)S(6)} %copy.23.count_ref, ...), custom_call_target="tpu_custom_call" | custom-call | tf_op jit(solution)/shard_map/pallas_call | solution.py:204
  144.2 1.0 copy-done.1
  145.2 1.0 copy-done.2
  146.2 0.7 copy-done.3
  147.0 0.1 convert_element_type.10
  147.2 1.9 reshape.97.refs_1_
  149.0 2.1 reshape.96.refs_0_
  151.1 1.4 reshape.98.refs_2_
  152.5 2.3 reshape.99.refs_3_
  154.9 1.0 copy-done
  155.8 85.7 %shard_map.137 = (f32[108,128]{1,0:T(8,128)S(1)}, f32[36,128]{1,0:T(8,128)S(1)}, f32[144,128]{1,0:T(8,128)S(1)}, f32[144,128]{1,0:T(8,128)S(1)}, f32[2,128]{1,0:T(2,128)S(1)}) custom-call(bf16[32,108,128]{2,1,0:T(8,128)(2,1)S(1)} %reshape.96.refs_0_, bf16[32,36,128]{2,1,0:T(8,128)(2,1)S(1)} %copy-done, bf16[32,144,128]{2,1,0:T(8,128)(2,1)S(1)} %reshape.98.refs_2_, ...), custom_call_target="tpu_custom_call" | custom-call | tf_op jit(solution)/shard_map/pallas_call | solution.py:438
  241.5 0.6 copy.24
  242.2 0.6 copy.25
  242.8 0.6 copy.26
  243.4 0.6 copy.27
  244.0 0.6 copy.28
  (20 shorter events, 0.1 us)
Async XLA Ops:
  40.3 2.9 %slice-start = ((bf16[32,464,128]{2,1,0:T(8,128)(2,1)}), bf16[32,108,128]{2,1,0:T(8,128)(2,1)S(1)}, s32[]{:S(2)}) async-start(bf16[32,464,128]{2,1,0:T(8,128)(2,1)} %shard_map.135), calls=%async_computation | async-start | bytes 1835008 | tf_op jit(solution)/shard_map/slice | solution.py:482
  44.2 1.6 copy-start.5
  47.2 0.7 copy-start.4
  144.2 1.0 copy-start.1
  145.2 1.0 copy-start.2
  146.2 0.7 copy-start.3
  154.8 1.0 copy-start
where the time goes:
time: 247 us; the launch traced here: 245 us
  Pallas kernels  217 us (88%)
  local copies, waits for them, and re-layouts  26 us (11%)
    pallas_call x1, Pallas kernels, run_layer(): pl.pallas_call(layer_kernel, grid_spec=pltpu.PrefetchScalarGridSpec(num_s...  96.3 us
    pallas_call x1, Pallas kernels, scatter_sum(): pl.pallas_call(lambda *refs: scatter_kernel(n_dp, n_y, len(terms), *refs)...  85.7 us
    pallas_call x1, Pallas kernels, gather_all(): pl.pallas_call(lambda *refs: gather_kernel(n_dp, n_y, len(parts), *refs),...  35 us
    reshape x5, local copies, waits for them, and re-layouts, to_rows(): return flat.reshape(count, lanes_of(size), LANES)  7.68 us
    unnamed x18, local copies, waits for them, and re-layouts  7.46 us

commit v1 on v0

--- a/solution.py
+++ b/solution.py
@@ -101,10 +101,10 @@
             cols = slice(pair * 2 * HEAD_DIM, (pair + 1) * 2 * HEAD_DIM)
             qp, kp, vp = qs[:, cols], ks[:, cols], vs[:, cols]
             both = None
+            twice = mm_t(jnp.concatenate([jnp.where(m, kp, zero) for m in halves], axis=0), qp)
             for h in range(2):
-                km = jnp.where(halves[h], kp, zero)
                 vm = jnp.where(halves[h], vp, zero)
-                scores = mm_t(km, qp)
+                scores = twice[h * rows : (h + 1) * rows]
                 scores = jnp.concatenate(
                     [scores[:whole_rows], jnp.where(keyrow < seq, scores[whole_rows:], -1e30)], axis=0
                 )
@@ -150,14 +150,14 @@
             cols = slice(pair * 2 * HEAD_DIM, (pair + 1) * 2 * HEAD_DIM)
             qp, kp, vp, dop = qs[:, cols], ks[:, cols], vs[:, cols], dos[:, cols]
             dq = dk = dv = None
+            twice = mm_t(jnp.concatenate([jnp.where(m, vp, zero) for m in halves], axis=0), dop)
             for h in range(2):
                 qm = jnp.where(halves[h], qp, zero)
                 km = jnp.where(halves[h], kp, zero)
-                vm = jnp.where(halves[h], vp, zero)
                 dom = jnp.where(halves[h], dop, zero)
                 pb = pbs[pair * 2 + h]
                 prob = pb.astype(F32)
-                dp = mm_t(vm, dop)
+                dp = twice[h * rows : (h + 1) * rows]
                 inner = jnp.sum(prob * dp, axis=0, keepdims=True)
                 ds = (prob * (dp - inner)).astype(BF16)
                 dv_h = mm(pb, dom)

time: 247 us -> 250 us (1.012)
  Pallas kernels: 217 us -> 221 us
    pallas_call x1, Pallas kernels: 85.7 us -> 95.3 us  [scatter_sum(): pl.pallas_call(lambda *refs: scatter_kernel(n_dp, n_y, len(terms), *refs)...]
    pallas_call x1, Pallas kernels: 96.3 us -> 90.3 us  [run_layer(): pl.pallas_call(layer_kernel, grid_spec=pltpu.PrefetchScalarGridSpec(num_s...]
where the time goes in v1:
time: 250 us; the launch traced here: 248 us
  Pallas kernels  221 us (88%)
  local copies, waits for them, and re-layouts  26 us (10%)
    pallas_call x1, Pallas kernels, scatter_sum(): pl.pallas_call(lambda *refs: scatter_kernel(n_dp, n_y, len(terms), *refs)...  95.3 us
    pallas_call x1, Pallas kernels, run_layer(): pl.pallas_call(layer_kernel, grid_spec=pltpu.PrefetchScalarGridSpec(num_s...  90.3 us
    pallas_call x1, Pallas kernels, gather_all(): pl.pallas_call(lambda *refs: gather_kernel(n_dp, n_y, len(parts), *refs),...  35 us
    reshape x5, local copies, waits for them, and re-layouts, to_rows(): return flat.reshape(count, lanes_of(size), LANES)  7.68 us
    unnamed x18, local copies, waits for them, and re-layouts  7.46 us

profile of v1, /device:TPU:11, one launch (start us, length us, event | category | flops | bytes accessed | tf_op | source)
XLA Modules:
  0.0 248.1 jit_solution(8935050753102046861)
XLA Ops:
  1.3 0.7 reshape.86
  1.9 0.5 pad_reduce_fusion
  2.5 35.0 %shard_map.135 = bf16[32,464,128]{2,1,0:T(8,128)(2,1)} custom-call(bf16[108,128]{1,0:T(8,128)(2,1)} %bitcast.26, bf16[36,128]{1,0:T(8,128)(2,1)} %bitcast.27, bf16[144,128]{1,0:T(8,128)(2,1)} %bitcast.23, bf16[144,128]{1,0:T(8,128)(2,1)} %bitcast.24, bf16[2,128]{1,0:T(2,128)(2,1)} %bitcast.28), custom_call_target="tpu_custom_call" | custom-call | tf_op jit(solution)/shard_map/pallas_call | solution.py:339
  37.5 0.9 slice.48
  38.4 0.1 reshape.108
  38.5 0.6 reshape.95.bup_ref
  39.1 1.0 slice.45
  40.1 0.2 reshape.88.wout_ref
  40.3 0.0 slice-start
  40.3 2.9 %fusion = (bf16[32,144,128]{2,1,0:T(8,128)(2,1)S(1)}, bf16[32,144,128]{2,1,0:T(8,128)(2,1)}) fusion(bf16[32,464,128]{2,1,0:T(8,128)(2,1)} %shard_map.135), kind=kLoop, calls=%fused_computation.7 | loop fusion | bytes 4718592 | tf_op jit(solution)/shard_map/slice | solution.py:482
  43.2 1.0 reshape.87.wqkv_ref
  44.2 0.0 copy-start.5
  44.2 1.6 reshape.90.wdown_ref
  45.8 1.4 reshape.89.wup_ref
  47.2 0.0 copy-start.4
  47.2 0.7 copy-done.4
  47.9 90.3 %shard_map.136 = (bf16[20,197,384]{2,1,0:T(8,128)(2,1)}, bf16[20,197,384]{2,1,0:T(8,128)(2,1)}, bf16[384,1152]{1,0:T(8,128)(2,1)S(1)}, bf16[384,384]{1,0:T(8,128...) custom-call(s32[1]{0:T(128)S(6)} %copy.23.count_ref, ...), custom_call_target="tpu_custom_call" | custom-call | tf_op jit(solution)/shard_map/pallas_call | solution.py:204
  138.1 1.0 copy-done.1
  139.1 1.0 copy-done.2
  140.1 0.7 copy-done.3
  140.9 0.1 convert_element_type.10
  141.1 1.9 reshape.97.refs_1_
  143.0 2.1 reshape.96.refs_0_
  145.0 1.4 reshape.98.refs_2_
  146.5 2.3 reshape.99.refs_3_
  148.8 1.0 copy-done
  149.7 95.3 %shard_map.137 = (f32[108,128]{1,0:T(8,128)S(1)}, f32[36,128]{1,0:T(8,128)S(1)}, f32[144,128]{1,0:T(8,128)S(1)}, f32[144,128]{1,0:T(8,128)S(1)}, f32[2,128]{1,0:T(2,128)S(1)}) custom-call(bf16[32,108,128]{2,1,0:T(8,128)(2,1)S(1)} %reshape.96.refs_0_, bf16[32,36,128]{2,1,0:T(8,128)(2,1)S(1)} %copy-done, bf16[32,144,128]{2,1,0:T(8,128)(2,1)S(1)} %reshape.98.refs_2_, ...), custom_call_target="tpu_custom_call" | custom-call | tf_op jit(solution)/shard_map/pallas_call | solution.py:438
  245.0 0.6 copy.24
  245.7 0.6 copy.25
  246.3 0.6 copy.26
  246.9 0.6 copy.27
  247.5 0.6 copy.28
  (20 shorter events, 0.1 us)
Async XLA Ops:
  40.3 2.9 %slice-start = ((bf16[32,464,128]{2,1,0:T(8,128)(2,1)}), bf16[32,108,128]{2,1,0:T(8,128)(2,1)S(1)}, s32[]{:S(2)}) async-start(bf16[32,464,128]{2,1,0:T(8,128)(2,1)} %shard_map.135), calls=%async_computation | async-start | bytes 1835008 | tf_op jit(solution)/shard_map/slice | solution.py:482
  44.2 1.6 copy-start.5
  47.2 0.7 copy-start.4
  138.1 1.0 copy-start.1
  139.1 1.0 copy-start.2
  140.1 0.7 copy-start.3
  148.8 1.0 copy-start
